TPU v7x, 32 devices: a whole 2x2x4 slice. The times are simulated.
32 devices in a mesh: grp: 2 (over y), freq: 4 (over z), tri: 2 (over x), sta: 2 (over core).
Axes of the slice: x: 2, y: 2, z: 4, core: 2. Of those that a mesh axis runs over, the one named last changes fastest.
Arguments:
- slip: float32 [8, 8192], P(None, ('grp', 'freq', 'tri')), parts along dimension 1, may hold values from 0 to 1
- green: float32 [32, 8, 64, 128], P('freq'), may hold values from -0.09375 to 0.09375
- pattern: int32 [64, 64], P('sta'), may hold values from -1 to 7
- observed: float32 [2, 64, 4096], P(None, ('grp', 'freq'), 'sta'), parts along dimension 1, may hold values from -6 to 6
- adjacency: int32 [3, 2048], P(None, ('freq', 'tri')), may hold values from 0 to 2047, as said below
- smooth_weight: float32 [2], P('grp'), parts along dimension 0, may hold values from 2 to 8
Outputs:
- new_slip: float32 [8, 8192], P(None, ('grp', 'freq', 'tri')), parts along dimension 1
- residual: float32 [2, 64, 4096], P(None, ('grp', 'freq'), 'sta'), parts along dimension 1
There are 2 independent parts, one for each index of `grp`. A program takes and returns all parts, laid end to end along the dimension named above; an argument that names none is the same for every part. Nothing has to cross between parts.
Inputs may be any that keep to these rules, and one draw needn't show every extreme that they name: adjacency[j, t] differs from t by 1 to 256, and adjacency[0, t] differs from t by exactly 256. `pattern`: -1 marks an absent block.
All inputs are finite; a program needn't handle non-finite values.
Results may differ from a plain program's by a relative error of at most 0.000058.
Values sent between devices are 32-bit elements; how exact they have to be, the bound alone decides.
No kernel may reach another device: no remote copies, remote signals or barrier semaphores. Data moves between devices by JAX's collectives and lax.ppermute only.
A program may use at most 64 MiB of HBM per device.

v0:
```python
import math
import jax
import jax.numpy as jnp
from jax import lax
from jax.sharding import PartitionSpec as P

PRECISE = lax.Precision.HIGHEST


def padded_2(shard, sides, width):
    for axis, dim in sides:
        peers, length = (lax.axis_size(axis), shard.shape[dim])
        up = [(i, (i + 1) % peers) for i in range(peers - 1)]
        down = [(j, i) for i, j in up]
        last = lax.slice_in_dim(shard, length - width, length, axis=dim)
        initial = lax.slice_in_dim(shard, 0, width, axis=dim)
        before = lax.ppermute(last, axis, up)
        after = lax.ppermute(initial, axis, down)
        shard = jnp.concatenate([before, shard, after], axis=dim)
    return shard


def phase_tables(first_freq, freq_count, freq_total, windows):
    frequency = jnp.arange(freq_count, dtype=jnp.float32) + first_freq + 1.0
    window = jnp.arange(windows, dtype=jnp.float32) + 0.5
    phases = 4.0 * math.pi / freq_total * frequency[:, None] * window[None, :]
    return (jnp.cos(phases), -jnp.sin(phases))


def apply_green(spectra, green, onehot, block):
    freqs = spectra.shape[1]
    columns = spectra.reshape(2, freqs, -1, block)
    summed = jnp.einsum("skc,rfcx->rfskx", onehot, columns, precision=PRECISE)
    green_real = green[:, :, :, :block]
    green_imag = green[:, :, :, block:]

    def product(left, right):
        return jnp.einsum("fkyx,fskx->fsy", left, right, precision=PRECISE)

    real_part = product(green_real, summed[0]) - product(green_imag, summed[1])
    imag_part = product(green_real, summed[1]) + product(green_imag, summed[0])
    return jnp.stack([real_part, imag_part]).reshape(2, freqs, -1)


def adjoint_green(misfit, green, onehot, block):
    freqs = misfit.shape[1]
    blocks = misfit.reshape(2, freqs, -1, block)
    green_real = green[:, :, :, :block]
    green_imag = green[:, :, :, block:]

    def product(left, right):
        return jnp.einsum("fkyx,fsy->fskx", left, right, precision=PRECISE)

    real_part = product(green_real, blocks[0]) + product(green_imag, blocks[1])
    imag_part = product(green_real, blocks[1]) - product(green_imag, blocks[0])
    result = jnp.einsum(
        "skc,rfskx->rfcx", onehot, jnp.stack([real_part, imag_part]), precision=PRECISE
    )
    return result.reshape(2, freqs, -1)


def local(slip, green, pattern, observed, adjacency, smooth_weight):
    smoothing = smooth_weight[0]
    n_freq = lax.axis_size("freq")
    n_tri = lax.axis_size("tri")
    freq_dev = green.shape[0]
    classes = green.shape[1]
    block = green.shape[2]
    freq_total = freq_dev * n_freq
    windows, columns = slip.shape
    tri_dev = columns // 2
    per_block = columns // block
    station_rows = pattern.shape[0]
    layout = pattern.reshape(station_rows, n_freq, n_tri, per_block)
    layout = lax.dynamic_index_in_dim(layout, lax.axis_index("tri"), 2, keepdims=False)
    layout = layout.reshape(station_rows, n_freq * per_block)
    onehot = (layout[:, None, :] == jnp.arange(classes, dtype=jnp.int32)[None, :, None]).astype(
        jnp.float32
    )
    cos_table, sin_table = phase_tables(0, freq_total, freq_total, windows)

    def to_spectra(field):
        spread = jnp.stack(
            [
                jnp.dot(cos_table, field, precision=PRECISE),
                jnp.dot(sin_table, field, precision=PRECISE),
            ]
        )
        return lax.all_to_all(spread, "freq", split_axis=1, concat_axis=2, tiled=True)

    def predict(field):
        partial_data = apply_green(to_spectra(field), green, onehot, block)
        return lax.psum(partial_data, "tri")

    predicted = predict(slip)
    residual = predicted - observed
    adjoint_part = adjoint_green(residual, green, onehot, block)
    adjoint_part = lax.psum(adjoint_part, "sta")
    by_frequency = lax.all_to_all(adjoint_part, "freq", split_axis=2, concat_axis=1, tiled=True)
    data_grad = jnp.dot(cos_table.T, by_frequency[0], precision=PRECISE) + jnp.dot(
        sin_table.T, by_frequency[1], precision=PRECISE
    )
    padded = padded_2(slip, ((("freq", "tri"), 1),), columns)
    padded_grid = padded.reshape(windows, 3 * tri_dev, 2)
    device_pos = lax.axis_index(("freq", "tri"))
    local_index = adjacency - (device_pos * tri_dev - tri_dev)
    picked = jnp.take(padded_grid, local_index, axis=1)
    neighbour_mean = (picked[:, 0] + picked[:, 1] + picked[:, 2]) / 3.0
    gradient = data_grad + smoothing * (slip - neighbour_mean.reshape(windows, columns))
    numerator = lax.psum(jnp.sum(gradient * gradient), ("freq", "tri"))
    image_data = predict(gradient)
    image_total = lax.psum(jnp.sum(image_data * image_data), ("freq", "sta"))
    denominator = image_total + smoothing * numerator
    step_length = numerator / denominator
    new_slip = jnp.maximum(slip - step_length * gradient, 0.0)
    return (new_slip, residual)


def solution(mesh):
    placed = (
        P(None, ("grp", "freq", "tri")),
        P("freq", None, None, None),
        P("sta", None),
        P(None, ("grp", "freq"), "sta"),
        P(None, ("freq", "tri")),
        P("grp"),
    )
    return jax.shard_map(
        local,
        mesh=mesh,
        in_specs=placed,
        out_specs=(P(None, ("grp", "freq", "tri")), P(None, ("grp", "freq"), "sta")),
        check_vma=False,
    )
```

profile of v0, /device:TPU:0, one launch (start us, length us, event | category | flops | bytes accessed | tf_op | source)
XLA Modules:
  0.0 188.8 jit_solution(9437272294900684459)
XLA Ops:
  7.2 5.0 %collective-permute-start = (f32[8,512]{1,0:T(8,128)}, f32[8,512]{1,0:T(8,128)S(1)}, u32[]{:S(2)}, u32[]{:S(2)}) collective-permute-start(f32[8,512]{1,0:T(8,128)} %param.6), channel_id=1, source_target_pairs={{0,2},{2,4},{4,6},{6,8},{8,10},{10,12},{12,14},{1,3},{3,5},{5,7},{... | collective-permute-start | bytes 49160 | tf_op jit(solution)/shard_map/ppermute | solution.py:17
  16.4 6.9 %all-to-all-start = ((f32[2,32,512]{2,0,1:T(2,128)}), f32[2,32,512]{2,0,1:T(2,128)S(1)}, u32[]{:S(2)}, u32[]{:S(2)}) async-start(f32[2,32,512]{2,0,1:T(2,128)} %copy.59), calls=%async_computation | async-start | bytes 262144 | tf_op jit(solution)/shard_map/all_to_all | solution.py:89
  26.2 3.1 %all-to-all-done = f32[2,32,512]{2,0,1:T(2,128)S(1)} async-done(((f32[2,32,512]{2,0,1:T(2,128)}), f32[2,32,512]{2,0,1:T(2,128)S(1)}, u32[]{:S(2)}, u32[]{:S(2)}) %all-to-all-start) | async-done | bytes 131104 | tf_op jit(solution)/shard_map/all_to_all | solution.py:89
  30.5 1.9 %fusion.43 = f32[8,32,64]{2,1,0:T(8,128)S(1)} fusion(f32[8,8,64,128]{3,2,1,0:T(8,128)S(1)} %copy-done, f32[2,8,32,8,64]{4,2,3,1,0:T(8,128)S(1)} %convolution_bitcast_fusion.1), kind=kOutput, calls=%fused_computation.36 | convolution fusion | flops 100663296 | bytes 3211264 | tf_op jit(solution)/shard_map/fkyx,fskx->fsy/dot_general | solution.py:38
  32.4 1.9 %fusion.46 = f32[8,32,64]{2,1,0:T(8,128)S(1)} fusion(f32[8,8,64,128]{3,2,1,0:T(8,128)S(1)} %copy-done, f32[2,8,32,8,64]{4,2,3,1,0:T(8,128)S(1)} %convolution_bitcast_fusion.1), kind=kOutput, calls=%fused_computation.37 | convolution fusion | flops 100663296 | bytes 3211264 | tf_op jit(solution)/shard_map/fkyx,fskx->fsy/dot_general | solution.py:38
  34.4 2.2 %fusion.76 = f32[8,32,64]{2,1,0:T(8,128)S(1)} fusion(f32[8,32,64]{2,1,0:T(8,128)S(1)} %fusion.43, f32[8,8,64,128]{3,2,1,0:T(8,128)S(1)} %copy-done, f32[2,8,32,8,64]{4,2,3,1,0:T(8,128)S(1)} %convolution_bitcast_fusion.1), kind=kOutput, calls=%fused_computation.47 | convolution fusion | flops 100679680 | bytes 3342336 | tf_op jit(solution)/shard_map/fkyx,fskx->fsy/dot_general | solution.py:38
  36.7 3.4 %fusion.73 = f32[8,32,64]{2,1,0:T(8,128)S(1)} fusion(f32[8,32,64]{2,1,0:T(8,128)S(1)} %fusion.46, f32[8,8,64,128]{3,2,1,0:T(8,128)S(1)} %copy-done, f32[2,8,32,8,64]{4,2,3,1,0:T(8,128)} %copy-done.2), kind=kOutput, calls=%fused_computation.46 | convolution fusion | flops 100679680 | bytes 3276800 | tf_op jit(solution)/shard_map/fkyx,fskx->fsy/dot_general | solution.py:38
  41.4 3.2 %gather_fusion = f32[768,8,2]{1,2,0:T(2,128)} fusion(f32[8,768,2]{0,2,1:T(2,128)S(1)} %bitcast.129, s32[1024]{0:T(1024)S(1)} %pad_clamp_fusion), kind=kCustom, calls=%fused_computation | custom fusion | bytes 101376 | tf_op jit(solution)/shard_map/jit(_take)/gather | solution.py:107
  44.6 1.9 copy.70
  46.5 14.1 %all-reduce.4.cloned.1.call-done = f32[2,8,2048]{2,1,0:T(8,128)} async-done(((f32[2,8,2048]{2,1,0:T(8,128)}), f32[2,8,2048]{2,1,0:T(8,128)}) %all-reduce.4.cloned.1.call-update) | async-done | bytes 131088 | tf_op jit(solution)/shard_map/psum | solution.py:93
  69.7 2.3 %copy.91 = f32[2,8,32,64]{1,0,3,2:T(2,128)} copy(f32[2,8,32,64]{3,2,1,0:T(8,128)S(1)} %fusion.40) | data formatting | bytes 262144 | tf_op jit(solution)/shard_map/reshape | solution.py:59
  72.1 21.3 %all-reduce.6.cloned.1.call-done = f32[2,8,2048]{1,0,2:T(2,128)} async-done(((f32[2,8,2048]{1,0,2:T(2,128)}), f32[2,8,2048]{1,0,2:T(2,128)}) %all-reduce.6.cloned.1.call-update) | async-done | bytes 131088 | tf_op jit(solution)/shard_map/psum | solution.py:98
  93.4 5.6 %reshape.99 = f32[4,1,8192]{2,1,0:T(1,128)} reshape(f32[2048,2,8]{2,1,0:T(2,128)} %bitcast.133) | data formatting | bytes 262144
  99.0 4.9 %all-to-all-start.1 = ((f32[4,1,8192]{2,1,0:T(1,128)}), f32[4,1,8192]{2,1,0:T(1,128)S(1)}, u32[]{:S(2)}, u32[]{:S(2)}) async-start(f32[4,1,8192]{2,1,0:T(1,128)} %reshape.99), calls=%async_computation.1 | async-start | bytes 262144 | tf_op jit(solution)/shard_map/all_to_all | solution.py:99
  104.1 6.1 %all-to-all-done.1 = f32[4,1,8192]{2,1,0:T(1,128)S(1)} async-done(((f32[4,1,8192]{2,1,0:T(1,128)}), f32[4,1,8192]{2,1,0:T(1,128)S(1)}, u32[]{:S(2)}, u32[]{:S(2)}) %all-to-all-start.1) | async-done | bytes 131104 | tf_op jit(solution)/shard_map/all_to_all | solution.py:99
  111.7 4.6 %reshape.100 = f32[2048,2,8]{2,1,0:T(2,128)} reshape(f32[4,8192]{1,0:T(4,128)S(1)} %reduce) | data formatting | bytes 262144
  116.3 2.6 %copy.92 = f32[2,8,4,512]{3,2,1,0:T(4,128)S(1)} copy(f32[2,8,4,512]{1,0,3,2:T(2,128)} %bitcast.132) | data formatting | bytes 262144 | tf_op jit(solution)/shard_map/all_to_all | solution.py:99
  121.0 8.6 %all_to_all.45 = f32[2,32,512]{2,0,1:T(2,128)S(1)} all-to-all(f32[2,32,512]{2,0,1:T(2,128)S(1)} %copy.73), channel_id=1, replica_groups=mesh['grp'=2,'freq'=4,'tri'=2,'sta'=2] {'freq'}, dimensions={1} | all-to-all | bytes 262144 | tf_op jit(solution)/shard_map/all_to_all | solution.py:89
  130.9 1.9 %fusion.49 = f32[8,32,64]{2,1,0:T(8,128)S(1)} fusion(f32[8,8,64,128]{3,2,1,0:T(8,128)S(1)} %copy-done, f32[2,8,32,8,64]{4,2,3,1,0:T(8,128)S(1)} %convolution_bitcast_fusion), kind=kOutput, calls=%fused_computation.38 | convolution fusion | flops 100663296 | bytes 3211264 | tf_op jit(solution)/shard_map/fkyx,fskx->fsy/dot_general | solution.py:38
  132.8 1.9 %fusion.52 = f32[8,32,64]{2,1,0:T(8,128)S(1)} fusion(f32[8,8,64,128]{3,2,1,0:T(8,128)S(1)} %copy-done, f32[2,8,32,8,64]{4,2,3,1,0:T(8,128)S(1)} %convolution_bitcast_fusion), kind=kOutput, calls=%fused_computation.39 | convolution fusion | flops 100663296 | bytes 3211264 | tf_op jit(solution)/shard_map/fkyx,fskx->fsy/dot_general | solution.py:38
  134.8 2.2 %fusion.70 = f32[8,32,64]{2,1,0:T(8,128)S(1)} fusion(f32[8,32,64]{2,1,0:T(8,128)S(1)} %fusion.49, f32[8,8,64,128]{3,2,1,0:T(8,128)S(1)} %copy-done, f32[2,8,32,8,64]{4,2,3,1,0:T(8,128)S(1)} %convolution_bitcast_fusion), kind=kOutput, calls=%fused_computation.45 | convolution fusion | flops 100679680 | bytes 3342336 | tf_op jit(solution)/shard_map/fkyx,fskx->fsy/dot_general | solution.py:38
  137.0 3.4 %fusion.67 = f32[8,32,64]{2,1,0:T(8,128)S(1)} fusion(f32[8,32,64]{2,1,0:T(8,128)S(1)} %fusion.52, f32[8,8,64,128]{3,2,1,0:T(8,128)S(1)} %copy-done, f32[2,8,32,8,64]{4,2,3,1,0:T(8,128)} %copy-done.1), kind=kOutput, calls=%fused_computation.44 | convolution fusion | flops 100679680 | bytes 3276800 | tf_op jit(solution)/shard_map/fkyx,fskx->fsy/dot_general | solution.py:38
  141.2 20.3 %psum.37 = f32[]{:T(128)} all-reduce(f32[]{:T(128)} %get-tuple-element.8), channel_id=1, replica_groups=mesh['grp'=2,'freq'=4,'tri'=2,'sta'=2] {'freq','tri'}, use_global_device_ids=true, to_apply=%region_3.4 | all-reduce | flops 1 | bytes 8 | tf_op jit(solution)/shard_map/psum | solution.py:110
  164.1 16.4 %psum.39 = f32[]{:T(128)} all-reduce(f32[]{:T(128)} %multiply_reduce_fusion), channel_id=1, replica_groups=mesh['grp'=2,'freq'=4,'tri'=2,'sta'=2] {'freq','sta'}, use_global_device_ids=true, to_apply=%region_6.7 | all-reduce | flops 1 | bytes 8 | tf_op jit(solution)/shard_map/psum | solution.py:112
  (88 shorter events, 26.5 us)
Async XLA Ops:
  7.2 23.3 %copy-start = (f32[8,8,64,128]{3,2,1,0:T(8,128)S(1)}, f32[8,8,64,128]{3,2,1,0:T(8,128)}, u32[]{:S(2)}) copy-start(f32[8,8,64,128]{3,2,1,0:T(8,128)} %param.7) | copy-start | bytes 6291460
  7.2 33.9 %collective-permute-start = (f32[8,512]{1,0:T(8,128)}, f32[8,512]{1,0:T(8,128)S(1)}, u32[]{:S(2)}, u32[]{:S(2)}) collective-permute-start(f32[8,512]{1,0:T(8,128)} %param.6), channel_id=1, source_target_pairs={{0,2},{2,4},{4,6},{6,8},{8,10},{10,12},{12,14},{1,3},{3,5},{5,7},{... | collective-permute-start | bytes 49160 | tf_op jit(solution)/shard_map/ppermute | solution.py:17
  12.2 28.9 %collective-permute-start.1 = (f32[8,512]{1,0:T(8,128)}, f32[8,512]{1,0:T(8,128)S(1)}, u32[]{:S(2)}, u32[]{:S(2)}) collective-permute-start(f32[8,512]{1,0:T(8,128)} %param.6), channel_id=1, source_target_pairs={{2,0},{4,2},{6,4},{8,6},{10,8},{12,10},{14,12},{3,1},{5,3},{7,5},{... | collective-permute-start | bytes 49160 | tf_op jit(solution)/shard_map/ppermute | solution.py:18
  13.5 1.1 copy-start.9
  13.5 1.1 copy-start.11
  16.4 12.8 %all-to-all-start = ((f32[2,32,512]{2,0,1:T(2,128)}), f32[2,32,512]{2,0,1:T(2,128)S(1)}, u32[]{:S(2)}, u32[]{:S(2)}) async-start(f32[2,32,512]{2,0,1:T(2,128)} %copy.59), calls=%async_computation | async-start | bytes 262144 | tf_op jit(solution)/shard_map/all_to_all | solution.py:89
  23.3 37.2 %all-reduce.4.cloned.1.call-start = ((), (), s32[]{:S(2)}) async-start(), calls=%async_computation.3 | async-start | bytes 262144 | tf_op jit(solution)/shard_map/psum | solution.py:93
  25.5 6.9 %copy-start.5 = (s32[32,32]{1,0:T(8,128)}, s32[32,32]{1,0:T(8,128)S(1)}, u32[]{:S(2)}) copy-start(s32[32,32]{1,0:T(8,128)S(1)} %copy.62) | copy-start | bytes 12292
  30.5 3.9 %copy-start.2 = (f32[2,8,32,8,64]{4,2,3,1,0:T(8,128)}, f32[2,8,32,8,64]{4,2,3,1,0:T(8,128)S(1)}, u32[]{:S(2)}) copy-start(f32[2,8,32,8,64]{4,2,3,1,0:T(8,128)S(1)} %convolution_bitcast_fusion.1) | copy-start | bytes 3145732
  36.6 4.5 %copy-start.4 = (f32[8,512]{1,0:T(8,128)S(1)}, f32[8,512]{1,0:T(8,128)}, u32[]{:S(2)}) copy-start(f32[8,512]{1,0:T(8,128)} %param.6) | copy-start | bytes 49156
  40.8 52.6 %all-reduce.6.cloned.1.call-start = ((), (), s32[]{:S(2)}) async-start(), calls=%async_computation.4 | async-start | bytes 4194304 | tf_op jit(solution)/shard_map/psum | solution.py:98
  41.4 19.2 %copy-start.8 = (f32[2,8,2048]{2,1,0:T(8,128)S(1)}, f32[2,8,2048]{2,1,0:T(8,128)}, u32[]{:S(2)}) copy-start(f32[2,8,2048]{2,1,0:T(8,128)} %param.9) | copy-start | bytes 393220
  61.5 4.8 %copy-start.3 = (f32[2,8,2048]{2,1,0:T(8,128)}, f32[2,8,2048]{2,1,0:T(8,128)S(1)}, u32[]{:S(2)}) copy-start(f32[2,8,2048]{2,1,0:T(8,128)S(1)} %sub.28) | copy-start | bytes 393220
  67.5 1.2 copy-start.6
  69.7 2.3 %copy-start.7 = (f32[3,256,8,2]{1,2,3,0:T(8,128)S(1)}, f32[3,256,8,2]{1,2,3,0:T(8,128)}, u32[]{:S(2)}) copy-start(f32[3,256,8,2]{1,2,3,0:T(8,128)} %copy.70) | copy-start | bytes 147460
  69.7 2.3 %copy-start.13 = (pred[3,256]{1,0:T(4,128)(4,1)S(1)}, pred[3,256]{1,0:T(4,128)(4,1)}, u32[]{:S(2)}) copy-start(pred[3,256]{1,0:T(4,128)(4,1)} %get-tuple-element.2) | copy-start | bytes 2308
  99.0 11.2 %all-to-all-start.1 = ((f32[4,1,8192]{2,1,0:T(1,128)}), f32[4,1,8192]{2,1,0:T(1,128)S(1)}, u32[]{:S(2)}, u32[]{:S(2)}) async-start(f32[4,1,8192]{2,1,0:T(1,128)} %reshape.99), calls=%async_computation.1 | async-start | bytes 262144 | tf_op jit(solution)/shard_map/all_to_all | solution.py:99
  103.8 58.1 %all-reduce.8.cloned.1.call-start = ((), (), s32[]{:S(2)}) async-start(), calls=%async_computation.5 | async-start | bytes 262144 | tf_op jit(solution)/shard_map/psum | solution.py:93
  111.7 7.3 %copy-start.10 = (f32[32]{0:T(128)S(1)}, f32[32]{0:T(128)}, u32[]{:S(2)}) copy-start(f32[32]{0:T(128)} %copy-done.9) | copy-start | bytes 388
  111.7 7.3 %copy-start.12 = (f32[8]{0:T(128)S(1)}, f32[8]{0:T(128)}, u32[]{:S(2)}) copy-start(f32[8]{0:T(128)} %copy-done.11) | copy-start | bytes 100
  130.9 3.9 %copy-start.1 = (f32[2,8,32,8,64]{4,2,3,1,0:T(8,128)}, f32[2,8,32,8,64]{4,2,3,1,0:T(8,128)S(1)}, u32[]{:S(2)}) copy-start(f32[2,8,32,8,64]{4,2,3,1,0:T(8,128)S(1)} %convolution_bitcast_fusion) | copy-start | bytes 3145732
Sparse Core Ops, SparseCore 0:
  40.9 19.5 all-reduce.3
  72.1 21.2 all-reduce.5
  141.3 20.5 all-reduce.7
where the time goes:
time: 190 us; the launch traced here: 189 us
  blocking collectives  45.3 us (24%)
  waiting for transfers between devices  45.1 us (24%)
  matrix products  31.2 us (16%)
  local copies, waits for them, and re-layouts  25.5 us (13%)
  starting transfers between devices  18.3 us (10%)
  between operations  16.7 us (9%)
  other arithmetic  6.71 us (4%)
    psum x1, waiting for transfers between devices, local(): adjoint_part = lax.psum(adjoint_part, 'sta')  21.3 us
    psum x1, blocking collectives, local(): numerator = lax.psum(jnp.sum(gradient * gradient), ('freq', 'tri'))  20.3 us
    dot_general x8, matrix products, product(): return jnp.einsum('fkyx,fskx->fsy', left, right, precision=PRECISE)  18.8 us
    psum x1, blocking collectives, local(): image_total = lax.psum(jnp.sum(image_data * image_data), ('freq', 'sta'))  16.4 us
    psum x2, waiting for transfers between devices, predict(): return lax.psum(partial_data, 'tri')  14.5 us
    unnamed x31, local copies, waits for them, and re-layouts  11 us
    all_to_all x1, blocking collectives, to_spectra(): lax.all_to_all(spread, 'freq', split_axis=1, concat_axis=2, tiled=True)  8.61 us
    all_to_all x1, starting transfers between devices, to_spectra(): lax.all_to_all(spread, 'freq', split_axis=1, concat_axis=2, tiled=True)  6.93 us
  transfers between devices with their start and end apart: 7, of which 5 were waited for; matrix products, arithmetic and copies ran while one was open for 12% of the time, Pallas kernels for 0%

commit v1 on v0

--- a/solution.py
+++ b/solution.py
@@ -95,7 +95,7 @@
     predicted = predict(slip)
     residual = predicted - observed
     adjoint_part = adjoint_green(residual, green, onehot, block)
-    adjoint_part = lax.psum(adjoint_part, "sta")
+    adjoint_part = jnp.sum(lax.all_gather(adjoint_part, "sta"), axis=0)
     by_frequency = lax.all_to_all(adjoint_part, "freq", split_axis=2, concat_axis=1, tiled=True)
     data_grad = jnp.dot(cos_table.T, by_frequency[0], precision=PRECISE) + jnp.dot(
         sin_table.T, by_frequency[1], precision=PRECISE

time: 190 us -> 173 us (0.911)
  waiting for transfers between devices: 45.1 us -> 28.1 us
    psum x1 -> x0, waiting for transfers between devices: 21.3 us -> none  [local(): adjoint_part = lax.psum(adjoint_part, 'sta')]
    psum x2, waiting for transfers between devices: 14.5 us -> 22.1 us  [predict(): return lax.psum(partial_data, 'tri')]
    all_to_all x1, waiting for transfers between devices: 3.07 us -> 0.01 us  [to_spectra(): lax.all_to_all(spread, 'freq', split_axis=1, concat_axis=2, tiled=True)]
    reshape x1 -> x0, local copies, waits for them, and re-layouts: 2.29 us -> none  [adjoint_green(): return result.reshape(2, freqs, -1)]
    reduce_sum x0 -> x1, local copies, waits for them, and re-layouts: none -> 2.25 us  [local(): adjoint_part = jnp.sum(lax.all_gather(adjoint_part, 'sta'), axis=0)]
    all_gather x0 -> x1, blocking collectives: none -> 1.99 us  [local(): adjoint_part = jnp.sum(lax.all_gather(adjoint_part, 'sta'), axis=0)]
    gather x2, local copies, waits for them, and re-layouts: 5.11 us -> 3.15 us  [local(): picked = jnp.take(padded_grid, local_index, axis=1)]
    unnamed x31 -> x25, local copies, waits for them, and re-layouts: 11 us -> 11 us
  transfers between devices with their start and end apart: 7 -> 6, of which waited for: 5 -> 3; matrix products, arithmetic and copies ran while one was open for 12% -> 6% of each run, Pallas kernels for 0% -> 0%
where the time goes in v1:
time: 173 us; the launch traced here: 172 us
  blocking collectives  46.2 us (27%)
  matrix products  31.5 us (18%)
  waiting for transfers between devices  28.1 us (16%)
  local copies, waits for them, and re-layouts  23.7 us (14%)
  starting transfers between devices  17.7 us (10%)
  between operations  17.1 us (10%)
  other arithmetic  7.51 us (4%)
    psum x2, waiting for transfers between devices, predict(): return lax.psum(partial_data, 'tri')  22.1 us
    psum x1, blocking collectives, local(): numerator = lax.psum(jnp.sum(gradient * gradient), ('freq', 'tri'))  19.2 us
    dot_general x8, matrix products, product(): return jnp.einsum('fkyx,fskx->fsy', left, right, precision=PRECISE)  18.9 us
    psum x1, blocking collectives, local(): image_total = lax.psum(jnp.sum(image_data * image_data), ('freq', 'sta'))  16.4 us
    unnamed x25, local copies, waits for them, and re-layouts  11 us
    all_to_all x1, blocking collectives, to_spectra(): lax.all_to_all(spread, 'freq', split_axis=1, concat_axis=2, tiled=True)  8.6 us
    all_to_all x1, starting transfers between devices, to_spectra(): lax.all_to_all(spread, 'freq', split_axis=1, concat_axis=2, tiled=True)  6.93 us
    all_to_all x1, waiting for transfers between devices, local(): lax.all_to_all(adjoint_part, 'freq', split_axis=2, concat_axis=1, tiled=T...  5.95 us
  transfers between devices with their start and end apart: 6, of which 3 were waited for; matrix products, arithmetic and copies ran while one was open for 6% of the time, Pallas kernels for 0%

profile of v1, /device:TPU:0, one launch (start us, length us, event | category | flops | bytes accessed | tf_op | source)
XLA Modules:
  0.0 171.8 jit_solution(1240194296911120453)
XLA Ops:
  7.2 4.8 %collective-permute-start = (f32[8,512]{1,0:T(8,128)}, f32[8,512]{1,0:T(8,128)S(1)}, u32[]{:S(2)}, u32[]{:S(2)}) collective-permute-start(f32[8,512]{1,0:T(8,128)} %param.6), channel_id=1, source_target_pairs={{0,2},{2,4},{4,6},{6,8},{8,10},{10,12},{12,14},{1,3},{3,5},{5,7},{... | collective-permute-start | bytes 49160 | tf_op jit(solution)/shard_map/ppermute | solution.py:17
  16.2 6.9 %all-to-all-start = ((f32[2,32,512]{2,0,1:T(2,128)}), f32[2,32,512]{2,0,1:T(2,128)S(1)}, u32[]{:S(2)}, u32[]{:S(2)}) async-start(f32[2,32,512]{2,0,1:T(2,128)} %copy.71), calls=%async_computation | async-start | bytes 262144 | tf_op jit(solution)/shard_map/all_to_all | solution.py:89
  26.4 2.8 %gather_fusion = f32[768,8,2]{1,2,0:T(2,128)S(1)} fusion(f32[8,768,2]{0,2,1:T(2,128)S(1)} %bitcast.130, s32[1024]{0:T(1024)S(1)} %pad_clamp_fusion), kind=kCustom, calls=%fused_computation | custom fusion | bytes 101376 | tf_op jit(solution)/shard_map/jit(_take)/gather | solution.py:107
  30.9 1.9 %fusion.43 = f32[8,32,64]{2,1,0:T(8,128)S(1)} fusion(f32[8,8,64,128]{3,2,1,0:T(8,128)S(1)} %copy-done, f32[2,8,32,8,64]{4,2,3,1,0:T(8,128)S(1)} %convolution_bitcast_fusion.1), kind=kOutput, calls=%fused_computation.36 | convolution fusion | flops 100663296 | bytes 3211264 | tf_op jit(solution)/shard_map/fkyx,fskx->fsy/dot_general | solution.py:38
  32.8 1.9 %fusion.46 = f32[8,32,64]{2,1,0:T(8,128)S(1)} fusion(f32[8,8,64,128]{3,2,1,0:T(8,128)S(1)} %copy-done, f32[2,8,32,8,64]{4,2,3,1,0:T(8,128)S(1)} %convolution_bitcast_fusion.1), kind=kOutput, calls=%fused_computation.37 | convolution fusion | flops 100663296 | bytes 3211264 | tf_op jit(solution)/shard_map/fkyx,fskx->fsy/dot_general | solution.py:38
  34.8 2.2 %fusion.76 = f32[8,32,64]{2,1,0:T(8,128)S(1)} fusion(f32[8,32,64]{2,1,0:T(8,128)S(1)} %fusion.43, f32[8,8,64,128]{3,2,1,0:T(8,128)S(1)} %copy-done, f32[2,8,32,8,64]{4,2,3,1,0:T(8,128)S(1)} %convolution_bitcast_fusion.1), kind=kOutput, calls=%fused_computation.47 | convolution fusion | flops 100679680 | bytes 3342336 | tf_op jit(solution)/shard_map/fkyx,fskx->fsy/dot_general | solution.py:38
  37.1 3.4 %fusion.73 = f32[8,32,64]{2,1,0:T(8,128)S(1)} fusion(f32[8,32,64]{2,1,0:T(8,128)S(1)} %fusion.46, f32[8,8,64,128]{3,2,1,0:T(8,128)S(1)} %copy-done, f32[2,8,32,8,64]{4,2,3,1,0:T(8,128)} %copy-done.2), kind=kOutput, calls=%fused_computation.46 | convolution fusion | flops 100679680 | bytes 3276800 | tf_op jit(solution)/shard_map/fkyx,fskx->fsy/dot_general | solution.py:38
  41.9 21.5 %all-reduce.3.cloned.1.call-done = f32[2,8,2048]{2,1,0:T(8,128)} async-done(((f32[2,8,2048]{2,1,0:T(8,128)}), f32[2,8,2048]{2,1,0:T(8,128)}) %all-reduce.3.cloned.1.call-update) | async-done | bytes 131088 | tf_op jit(solution)/shard_map/psum | solution.py:93
  67.6 1.6 fusion.8
  72.8 2.0 %all_gather.3 = f32[2,2,8,2048]{3,2,1,0:T(8,128)S(1)} all-gather(f32[1,2,8,2048]{3,2,1,0:T(8,128)S(1)} %all_gather_reshape.3), channel_id=1, replica_groups=mesh['grp'=2,'freq'=4,'tri'=2,'sta'=2] {'sta'}, dimensions={0}, use_global_device_ids=true | all-gather | bytes 393216 | tf_op jit(solution)/shard_map/all_gather | solution.py:98
  74.8 2.2 %copy.76 = f32[2,8,2048]{1,0,2:T(2,128)} copy(f32[2,8,2048]{2,1,0:T(8,128)S(1)} %reduce_sum.27) | data formatting | bytes 262144 | tf_op jit(solution)/shard_map/reduce_sum | solution.py:98
  77.1 5.6 %reshape.95 = f32[4,1,8192]{2,1,0:T(1,128)} reshape(f32[2048,2,8]{2,1,0:T(2,128)} %bitcast.132) | data formatting | bytes 262144
  82.6 4.6 %all-to-all-start.1 = ((f32[4,1,8192]{2,1,0:T(1,128)}), f32[4,1,8192]{2,1,0:T(1,128)S(1)}, u32[]{:S(2)}, u32[]{:S(2)}) async-start(f32[4,1,8192]{2,1,0:T(1,128)} %reshape.95), calls=%async_computation.1 | async-start | bytes 262144 | tf_op jit(solution)/shard_map/all_to_all | solution.py:99
  87.5 5.9 %all-to-all-done.1 = f32[4,1,8192]{2,1,0:T(1,128)S(1)} async-done(((f32[4,1,8192]{2,1,0:T(1,128)}), f32[4,1,8192]{2,1,0:T(1,128)S(1)}, u32[]{:S(2)}, u32[]{:S(2)}) %all-to-all-start.1) | async-done | bytes 131104 | tf_op jit(solution)/shard_map/all_to_all | solution.py:99
  95.0 4.5 %reshape.96 = f32[2048,2,8]{2,1,0:T(2,128)} reshape(f32[4,8192]{1,0:T(4,128)S(1)} %reduce) | data formatting | bytes 262144
  99.5 2.6 %copy.103 = f32[2,8,4,512]{3,2,1,0:T(4,128)S(1)} copy(f32[2,8,4,512]{1,0,3,2:T(2,128)} %bitcast.133) | data formatting | bytes 262144 | tf_op jit(solution)/shard_map/all_to_all | solution.py:99
  104.4 8.6 %all_to_all.45 = f32[2,32,512]{2,0,1:T(2,128)S(1)} all-to-all(f32[2,32,512]{2,0,1:T(2,128)S(1)} %copy.85), channel_id=1, replica_groups=mesh['grp'=2,'freq'=4,'tri'=2,'sta'=2] {'freq'}, dimensions={1} | all-to-all | bytes 262144 | tf_op jit(solution)/shard_map/all_to_all | solution.py:89
  114.2 1.9 %fusion.49 = f32[8,32,64]{2,1,0:T(8,128)S(1)} fusion(f32[8,8,64,128]{3,2,1,0:T(8,128)S(1)} %copy-done, f32[2,8,32,8,64]{4,2,3,1,0:T(8,128)S(1)} %convolution_bitcast_fusion), kind=kOutput, calls=%fused_computation.38 | convolution fusion | flops 100663296 | bytes 3211264 | tf_op jit(solution)/shard_map/fkyx,fskx->fsy/dot_general | solution.py:38
  116.1 1.9 %fusion.52 = f32[8,32,64]{2,1,0:T(8,128)S(1)} fusion(f32[8,8,64,128]{3,2,1,0:T(8,128)S(1)} %copy-done, f32[2,8,32,8,64]{4,2,3,1,0:T(8,128)S(1)} %convolution_bitcast_fusion), kind=kOutput, calls=%fused_computation.39 | convolution fusion | flops 100663296 | bytes 3211264 | tf_op jit(solution)/shard_map/fkyx,fskx->fsy/dot_general | solution.py:38
  118.1 2.2 %fusion.70 = f32[8,32,64]{2,1,0:T(8,128)S(1)} fusion(f32[8,32,64]{2,1,0:T(8,128)S(1)} %fusion.49, f32[8,8,64,128]{3,2,1,0:T(8,128)S(1)} %copy-done, f32[2,8,32,8,64]{4,2,3,1,0:T(8,128)S(1)} %convolution_bitcast_fusion), kind=kOutput, calls=%fused_computation.45 | convolution fusion | flops 100679680 | bytes 3342336 | tf_op jit(solution)/shard_map/fkyx,fskx->fsy/dot_general | solution.py:38
  120.4 3.4 %fusion.67 = f32[8,32,64]{2,1,0:T(8,128)S(1)} fusion(f32[8,32,64]{2,1,0:T(8,128)S(1)} %fusion.52, f32[8,8,64,128]{3,2,1,0:T(8,128)S(1)} %copy-done, f32[2,8,32,8,64]{4,2,3,1,0:T(8,128)} %copy-done.1), kind=kOutput, calls=%fused_computation.44 | convolution fusion | flops 100679680 | bytes 3276800 | tf_op jit(solution)/shard_map/fkyx,fskx->fsy/dot_general | solution.py:38
  124.5 19.2 %psum.29 = f32[]{:T(128)} all-reduce(f32[]{:T(128)} %get-tuple-element.8), channel_id=1, replica_groups=mesh['grp'=2,'freq'=4,'tri'=2,'sta'=2] {'freq','tri'}, use_global_device_ids=true, to_apply=%region_3.4 | all-reduce | flops 1 | bytes 8 | tf_op jit(solution)/shard_map/psum | solution.py:110
  144.3 1.6 multiply_reduce_fusion
  146.6 16.4 %psum.31 = f32[]{:T(128)} all-reduce(f32[]{:T(128)} %multiply_reduce_fusion), channel_id=1, replica_groups=mesh['grp'=2,'freq'=4,'tri'=2,'sta'=2] {'freq','sta'}, use_global_device_ids=true, to_apply=%region_6.7 | all-reduce | flops 1 | bytes 8 | tf_op jit(solution)/shard_map/psum | solution.py:112
  (82 shorter events, 24.7 us)
Async XLA Ops:
  7.2 18.3 %collective-permute-start = (f32[8,512]{1,0:T(8,128)}, f32[8,512]{1,0:T(8,128)S(1)}, u32[]{:S(2)}, u32[]{:S(2)}) collective-permute-start(f32[8,512]{1,0:T(8,128)} %param.6), channel_id=1, source_target_pairs={{0,2},{2,4},{4,6},{6,8},{8,10},{10,12},{12,14},{1,3},{3,5},{5,7},{... | collective-permute-start | bytes 49160 | tf_op jit(solution)/shard_map/ppermute | solution.py:17
  12.0 13.4 %collective-permute-start.1 = (f32[8,512]{1,0:T(8,128)}, f32[8,512]{1,0:T(8,128)S(1)}, u32[]{:S(2)}, u32[]{:S(2)}) collective-permute-start(f32[8,512]{1,0:T(8,128)} %param.6), channel_id=1, source_target_pairs={{2,0},{4,2},{6,4},{8,6},{10,8},{12,10},{14,12},{3,1},{5,3},{7,5},{... | collective-permute-start | bytes 49160 | tf_op jit(solution)/shard_map/ppermute | solution.py:18
  13.3 1.1 copy-start.7
  13.4 1.1 copy-start.9
  16.2 13.4 %all-to-all-start = ((f32[2,32,512]{2,0,1:T(2,128)}), f32[2,32,512]{2,0,1:T(2,128)S(1)}, u32[]{:S(2)}, u32[]{:S(2)}) async-start(f32[2,32,512]{2,0,1:T(2,128)} %copy.71), calls=%async_computation | async-start | bytes 262144 | tf_op jit(solution)/shard_map/all_to_all | solution.py:89
  23.2 40.2 %all-reduce.3.cloned.1.call-start = ((), (), s32[]{:S(2)}) async-start(), calls=%async_computation.3 | async-start | bytes 262144 | tf_op jit(solution)/shard_map/psum | solution.py:93
  29.3 1.6 copy-start
  30.9 3.9 %copy-start.2 = (f32[2,8,32,8,64]{4,2,3,1,0:T(8,128)}, f32[2,8,32,8,64]{4,2,3,1,0:T(8,128)S(1)}, u32[]{:S(2)}) copy-start(f32[2,8,32,8,64]{4,2,3,1,0:T(8,128)S(1)} %convolution_bitcast_fusion.1) | copy-start | bytes 3145732
  37.1 26.4 %copy-start.6 = (f32[2,8,2048]{2,1,0:T(8,128)S(1)}, f32[2,8,2048]{2,1,0:T(8,128)}, u32[]{:S(2)}) copy-start(f32[2,8,2048]{2,1,0:T(8,128)} %param.9) | copy-start | bytes 393220
  64.3 4.8 %copy-start.3 = (f32[2,8,2048]{2,1,0:T(8,128)}, f32[2,8,2048]{2,1,0:T(8,128)S(1)}, u32[]{:S(2)}) copy-start(f32[2,8,2048]{2,1,0:T(8,128)S(1)} %sub.28) | copy-start | bytes 393220
  74.8 12.4 %copy-start.5 = (f32[8,3,256,2]{2,0,3,1:T(8,128)S(1)}, f32[8,3,256,2]{2,0,3,1:T(8,128)}, u32[]{:S(2)}) copy-start(f32[8,3,256,2]{2,0,3,1:T(8,128)} %select_bitcast_fusion) | copy-start | bytes 147460
  82.6 10.8 %all-to-all-start.1 = ((f32[4,1,8192]{2,1,0:T(1,128)}), f32[4,1,8192]{2,1,0:T(1,128)S(1)}, u32[]{:S(2)}, u32[]{:S(2)}) async-start(f32[4,1,8192]{2,1,0:T(1,128)} %reshape.95), calls=%async_computation.1 | async-start | bytes 262144 | tf_op jit(solution)/shard_map/all_to_all | solution.py:99
  87.2 57.0 %all-reduce.5.cloned.1.call-start = ((), (), s32[]{:S(2)}) async-start(), calls=%async_computation.4 | async-start | bytes 262144 | tf_op jit(solution)/shard_map/psum | solution.py:93
  94.9 7.3 %copy-start.8 = (f32[32]{0:T(128)S(1)}, f32[32]{0:T(128)}, u32[]{:S(2)}) copy-start(f32[32]{0:T(128)} %copy-done.7) | copy-start | bytes 388
  95.0 7.3 %copy-start.10 = (f32[8]{0:T(128)S(1)}, f32[8]{0:T(128)}, u32[]{:S(2)}) copy-start(f32[8]{0:T(128)} %copy-done.9) | copy-start | bytes 100
  95.0 7.6 %copy-start.4 = (f32[8,512]{1,0:T(8,128)S(1)}, f32[8,512]{1,0:T(8,128)}, u32[]{:S(2)}) copy-start(f32[8,512]{1,0:T(8,128)} %param.6) | copy-start | bytes 49156
  114.2 3.9 %copy-start.1 = (f32[2,8,32,8,64]{4,2,3,1,0:T(8,128)}, f32[2,8,32,8,64]{4,2,3,1,0:T(8,128)S(1)}, u32[]{:S(2)}) copy-start(f32[2,8,32,8,64]{4,2,3,1,0:T(8,128)S(1)} %convolution_bitcast_fusion) | copy-start | bytes 3145732
Sparse Core Ops, SparseCore 0:
  41.4 21.9 all-reduce.2
  124.6 19.6 all-reduce.4
